TPU v7x, 32 devices: a whole 2x2x4 slice. The times are simulated.
32 devices in a mesh: parts: 2 (over y), context: 16 (over z, x, core).
Axes of the slice: x: 2, y: 2, z: 4, core: 2. Of those that a mesh axis runs over, the one named last changes fastest.
Arguments:
- projected: bfloat16 [4096, 12288], P(('parts', 'context')), parts along dimension 0, may hold values from -6 to 6
- short_taps: float32 [3, 12288], replicated, may hold values from -3.5 to 3.5
- residues: float32 [4096, 16], replicated, may hold values from -1.5 to 1.5
- rates: float32 [4096, 16], replicated, may hold values from 9.765625e-06 to 0.05
- skip: float32 [4096], replicated, may hold values from 0.5 to 1.5
Outputs:
- gated: bfloat16 [4096, 4096], P(('parts', 'context')), parts along dimension 0
There are 2 independent parts, one for each index of `parts`. A program takes and returns all parts, laid end to end along the dimension named above; an argument that names none is the same for every part. Nothing has to cross between parts.
All inputs are finite; a program needn't handle non-finite values.
Results may differ from a plain program's by a relative error of at most 0.0057.
Values may be sent and summed in bfloat16 or wider, within the bound.
A program may use at most 128 MiB of HBM per device.

v0:
```python
import functools

import jax
import jax.numpy as jnp
from jax import lax
from jax.experimental import pallas as pl
from jax.experimental.pallas import tpu as pltpu
from jax.sharding import PartitionSpec as P

SHORT = 3
LANES = 128
SUB = 8
TILE = SUB * LANES
MESH = pl.DeviceIdType.MESH
F32 = jnp.float32
BF16 = jnp.bfloat16


def one_less_exp(x):
    series = x * (
        1.0
        - x * (1 / 2) * (1.0 - x * (1 / 3) * (1.0 - x * (1 / 4) * (1.0 - x * (1 / 5) * (1.0 - x * (1 / 6)))))
    )
    return jnp.where(x < 0.125, series, 1.0 - jnp.exp(-x))


def tree_sum(values):
    values = list(values)
    while len(values) > 1:
        paired = [values[k] + values[k + 1] for k in range(0, len(values) - 1, 2)]
        if len(values) % 2:
            paired.append(values[-1])
        values = paired
    return values[0]


def kernel(
    n, rows, groups, modes,
    proj, taps, res, rate, skip, out,
    pin, rim, rim_f, rim_out, rim_in, px, z, y, pout, av, cv, dkv, tv,
    sent, got, back, carry,
    in_sems, rim_sem, out_sems, halo_send, halo_recv, send1, recv1, send2, recv2,
):
    me = lax.axis_index("context")
    tiles = groups // SUB
    share = modes * groups // n

    barrier = pltpu.get_barrier_semaphore()

    def greet(k, c):
        pl.semaphore_signal(
            barrier, inc=1, device_id={"context": lax.rem(me + k, n)}, device_id_type=MESH
        )
        return c

    lax.fori_loop(1, n, greet, 0)

    rim_copy = pltpu.make_async_copy(proj.at[pl.ds(rows - 16, 16), :], rim, rim_sem)
    rim_copy.start()

    def tile_copy(i):
        return pltpu.make_async_copy(
            proj.at[:, pl.ds(pl.multiple_of(i * TILE, TILE), TILE)], pin.at[i], in_sems.at[i]
        )

    def start_in(i, c):
        tile_copy(i).start()
        return c

    lax.fori_loop(0, 3 * tiles, start_in, 0)

    rim_copy.wait()

    def cut_rim(i, c):
        for j in range(SUB):
            cols = rim[:, pl.ds(pl.multiple_of(i * TILE + j * LANES, LANES), LANES)].astype(F32)
            rim_f[pl.ds(i * 16 + j, 2, stride=SUB), :] = cols[14:16]
        return c

    lax.fori_loop(0, 3 * tiles, cut_rim, 0)
    rim_out[...] = rim_f[...].astype(BF16)
    pl.semaphore_wait(barrier, n - 1)
    halo = pltpu.make_async_remote_copy(
        src_ref=rim_out,
        dst_ref=rim_in,
        send_sem=halo_send,
        recv_sem=halo_recv,
        device_id={"context": lax.rem(me + 1, n)},
        device_id_type=MESH,
    )

    @pl.when(me < n - 1)
    def _():
        halo.start()

    def params(j, c):
        cols = pl.ds(pl.multiple_of(j * LANES, LANES), LANES)
        r = rate[:, cols]
        where = pl.ds(j, modes, stride=groups)
        av[where, :] = jnp.exp(-r)
        dkv[where, :] = jnp.exp(-float(rows) * r)
        cv[where, :] = res[:, cols] * jnp.sqrt(one_less_exp(2.0 * r))
        return c

    lax.fori_loop(0, groups, params, 0)

    def set_taps(j, c):
        cols = pl.ds(pl.multiple_of(j * LANES, LANES), LANES)
        tv[pl.ds(j, SHORT, stride=3 * groups), :] = taps[:, cols]
        return c

    lax.fori_loop(0, 3 * groups, set_taps, 0)

    def spread(i, c):
        tile_copy(i).wait()
        for j in range(SUB):
            px[i, pl.ds(2 * SUB + j, rows, stride=SUB), :] = pin[
                i, :, j * LANES : (j + 1) * LANES
            ].astype(F32)
        return c

    lax.fori_loop(0, 3 * tiles, spread, 0)

    @pl.when(me < n - 1)
    def _():
        halo.wait_send()

    @pl.when(me > 0)
    def _():
        halo.wait_recv()

    @pl.when(me == 0)
    def _():
        rim_in[...] = jnp.zeros_like(rim_in)

    for i in range(3 * tiles):
        px[i, 0 : 2 * SUB, :] = rim_in[i * 16 : i * 16 + 16, :].astype(F32)

    def part(ref, m, i):
        return ref[pl.ds(pl.multiple_of(m * groups + i * SUB, SUB), SUB), :]

    def taps_of(stream, i):
        return [part(tv, 3 * k + stream, i) for k in range(SHORT)]

    def pre(tap, stream, i, t):
        total = None
        for k in range(SHORT):
            row = pl.multiple_of((t + SHORT - 1 - k) * SUB, SUB)
            term = tap[k] * px[stream * tiles + i, pl.ds(row, SUB), :]
            total = term if total is None else total + term
        return total

    def at(t):
        return pl.ds(pl.multiple_of(t * SUB, SUB), SUB)

    def put_state(ref, m, i, value):
        if share >= SUB:
            per = groups // share
            ref[m * per + (i * SUB) // share, pl.ds(pl.multiple_of((i * SUB) % share, SUB), SUB), :] = value
        else:
            count = SUB // share
            for k in range(count):
                ref[(m * groups + i * SUB) // share + k] = value[k * share : (k + 1) * share]

    def get_state(ref, m, i):
        if share >= SUB:
            per = groups // share
            return ref[m * per + (i * SUB) // share, pl.ds(pl.multiple_of((i * SUB) % share, SUB), SUB), :]
        count = SUB // share
        return jnp.concatenate(
            [ref[(m * groups + i * SUB) // share + k] for k in range(count)], axis=0
        )

    zeros = tuple(jnp.zeros((SUB, LANES), F32) for _ in range(modes))

    def end_states(i, c):
        a = [part(av, m, i) for m in range(modes)]
        tap2, tap3 = taps_of(1, i), taps_of(2, i)

        def step(t, h):
            zt = (pre(tap2, 1, i, t) * pre(tap3, 2, i, t)).astype(BF16).astype(F32)
            z[i, at(t), :] = zt
            return tuple(a[m] * h[m] + zt for m in range(modes))

        h = lax.fori_loop(0, rows, step, zeros, unroll=4)
        for m in range(modes):
            put_state(sent, m, i, h[m])
        return c

    lax.fori_loop(0, tiles, end_states, 0)

    def exchange(src, dst, send_sem, recv_sem):
        def one(k, c):
            other = lax.rem(me + k, n)
            pltpu.make_async_remote_copy(
                src_ref=src.at[other],
                dst_ref=dst.at[me],
                send_sem=send_sem,
                recv_sem=recv_sem,
                device_id={"context": other},
                device_id_type=MESH,
            ).start()
            return c

        lax.fori_loop(1, n, one, 0)
        dst[me] = src[me]

    def finish(src, dst, send_sem, recv_sem):
        most = pl.ds(0, n - 1)
        pltpu.make_async_copy(src.at[most], src.at[most], send_sem).wait()
        pltpu.make_async_copy(dst.at[most], dst.at[most], recv_sem).wait()

    exchange(sent, got, send1, recv1)

    def local(i, c):
        a = [part(av, m, i) for m in range(modes)]
        coef = [part(cv, m, i) for m in range(modes)]
        direct = part(skip, 0, i)

        def step(t, h):
            zt = z[i, at(t), :]
            h = tuple(a[m] * h[m] + zt for m in range(modes))
            y[i, at(t), :] = direct * zt + tree_sum(coef[m] * h[m] for m in range(modes))
            return h

        lax.fori_loop(0, rows, step, zeros, unroll=4)
        return c

    lax.fori_loop(0, tiles // 2, local, 0)
    finish(sent, got, send1, recv1)

    decay = dkv[pl.ds(me * share, share), :]

    def scan(d, held):
        back[d] = held
        return decay * held + got[d]

    lax.fori_loop(0, n, scan, jnp.zeros((share, LANES), F32))
    exchange(back, carry, send2, recv2)
    lax.fori_loop(tiles // 2, tiles, local, 0)
    finish(back, carry, send2, recv2)

    def out_copy(i):
        return pltpu.make_async_copy(
            pout.at[i], out.at[:, pl.ds(pl.multiple_of(i * TILE, TILE), TILE)], out_sems.at[i]
        )

    def close(i, c):
        a = [part(av, m, i) for m in range(modes)]
        tap1 = taps_of(0, i)
        g = tuple(part(cv, m, i) * get_state(carry, m, i) for m in range(modes))

        def step(t, g):
            g = tuple(a[m] * g[m] for m in range(modes))
            mixed = (y[i, at(t), :] + tree_sum(g)).astype(BF16).astype(F32)
            y[i, at(t), :] = pre(tap1, 0, i, t) * mixed
            return g

        lax.fori_loop(0, rows, step, g, unroll=4)
        for j in range(SUB):
            pout[i, :, j * LANES : (j + 1) * LANES] = y[
                i, pl.ds(j, rows, stride=SUB), :
            ].astype(BF16)
        out_copy(i).start()
        return c

    lax.fori_loop(0, tiles, close, 0)

    def end_out(i, c):
        out_copy(i).wait()
        return c

    lax.fori_loop(0, tiles, end_out, 0)


def per_device(projected, short_taps, residues, rates, skip):
    n = lax.axis_size("context")
    rows, width = projected.shape
    channels = width // 3
    modes = residues.shape[1]
    groups = channels // LANES
    tiles = channels // TILE
    share = modes * groups // n
    vmem = pl.BlockSpec(memory_space=pltpu.VMEM)
    hbm = pl.BlockSpec(memory_space=pl.ANY)
    dma = pltpu.SemaphoreType.DMA
    states = pltpu.VMEM((n, share, LANES), F32)
    flat = pltpu.VMEM((modes * groups, LANES), F32)
    return pl.pallas_call(
        functools.partial(kernel, n, rows, groups, modes),
        out_shape=jax.ShapeDtypeStruct((rows, channels), BF16),
        in_specs=[hbm, vmem, vmem, vmem, vmem],
        out_specs=hbm,
        scratch_shapes=[
            pltpu.VMEM((3 * tiles, rows, TILE), BF16),
            pltpu.VMEM((16, width), BF16),
            pltpu.VMEM((3 * tiles * 16, LANES), F32),
            pltpu.VMEM((3 * tiles * 16, LANES), BF16),
            pltpu.VMEM((3 * tiles * 16, LANES), BF16),
            pltpu.VMEM((3 * tiles, (rows + 2) * SUB, LANES), F32),
            pltpu.VMEM((tiles, rows * SUB, LANES), F32),
            pltpu.VMEM((tiles, rows * SUB, LANES), F32),
            pltpu.VMEM((tiles, rows, TILE), BF16),
            flat,
            flat,
            flat,
            pltpu.VMEM((SHORT * 3 * groups, LANES), F32),
            states,
            states,
            states,
            states,
            dma((3 * tiles,)),
            dma,
            dma((tiles,)),
            dma,
            dma,
            dma,
            dma,
            dma,
            dma,
        ],
        compiler_params=pltpu.CompilerParams(
            collective_id=0, has_side_effects=True, vmem_limit_bytes=48 * 1024 * 1024
        ),
        cost_estimate=pl.CostEstimate(
            flops=rows * channels * modes * 8, bytes_accessed=rows * channels * 8, transcendentals=0
        ),
    )(projected, short_taps, residues.T, rates.T, skip.reshape(groups, LANES))


def solution(mesh):
    in_specs = (P(("parts", "context"), None), P(), P(), P(), P())
    out_specs = P(("parts", "context"), None)
    return jax.shard_map(
        per_device, mesh=mesh, in_specs=in_specs, out_specs=out_specs, check_vma=False
    )
```

profile of v0, /device:TPU:0, one launch (start us, length us, event | category | flops | bytes accessed | tf_op | source)
XLA Modules:
  0.0 36.2 jit_solution(2469752374294807220)
XLA Ops:
  0.0 0.0 copy-start
  0.0 1.9 %copy-done = bf16[128,12288]{1,0:T(8,128)(2,1)S(1)} copy-done((bf16[128,12288]{1,0:T(8,128)(2,1)S(1)}, bf16[128,12288]{1,0:T(8,128)(2,1)}, u32[]{:S(2)}) %copy-start) | copy-done | bytes 3145752
  1.9 0.0 copy-start.1
  1.9 0.9 %copy-done.1 = f32[4096,16]{0,1:T(8,128)S(1)} copy-done((f32[4096,16]{0,1:T(8,128)S(1)}, f32[4096,16]{0,1:T(8,128)}, u32[]{:S(2)}) %copy-start.1) | copy-done | bytes 262168
  2.8 0.0 copy-start.2
  2.8 0.9 %copy-done.2 = f32[4096,16]{0,1:T(8,128)S(1)} copy-done((f32[4096,16]{0,1:T(8,128)S(1)}, f32[4096,16]{0,1:T(8,128)}, u32[]{:S(2)}) %copy-start.2) | copy-done | bytes 262168
  3.8 0.0 copy-start.3
  3.8 0.9 %copy-done.3 = f32[3,12288]{1,0:T(4,128)S(1)} copy-done((f32[3,12288]{1,0:T(4,128)S(1)}, f32[3,12288]{1,0:T(4,128)}, u32[]{:S(2)}) %copy-start.3) | copy-done | bytes 147480
  4.7 0.0 copy-start.4
  4.7 0.7 %copy-done.4 = f32[4096]{0:T(1024)S(1)} copy-done((f32[4096]{0:T(1024)S(1)}, f32[4096]{0:T(1024)}, u32[]{:S(2)}) %copy-start.4) | copy-done | bytes 16408
  5.4 29.8 %shard_map.55 = bf16[128,4096]{1,0:T(8,128)(2,1)S(1)} custom-call(bf16[128,12288]{1,0:T(8,128)(2,1)S(1)} %copy-done, f32[3,12288]{1,0:T(4,128)S(1)} %copy-done.3, f32[16,4096]{1,0:T(8,128)S(1)} %bitcast.3, f32[16,4096]{1,0:T(8,128)S(1)} %bitcast.4, f32[32,128]{1,0:T(8,128)S(1)} %bitcast.5), custom_call_target="tpu_custom_call" | custom-call | flops 67108864 | bytes 4194304 | tf_op jit(solution)/shard_map/pallas_call | solution.py:289
  35.3 1.0 %copy.7 = bf16[128,4096]{1,0:T(8,128)(2,1)} copy(bf16[128,4096]{1,0:T(8,128)(2,1)S(1)} %shard_map.55) | data formatting | bytes 2097152
Async XLA Ops:
  0.0 1.9 %copy-start = (bf16[128,12288]{1,0:T(8,128)(2,1)S(1)}, bf16[128,12288]{1,0:T(8,128)(2,1)}, u32[]{:S(2)}) copy-start(bf16[128,12288]{1,0:T(8,128)(2,1)} %proj.1) | copy-start | bytes 9437188
  1.9 0.9 %copy-start.1 = (f32[4096,16]{0,1:T(8,128)S(1)}, f32[4096,16]{0,1:T(8,128)}, u32[]{:S(2)}) copy-start(f32[4096,16]{0,1:T(8,128)} %param.7) | copy-start | bytes 786436
  2.8 0.9 %copy-start.2 = (f32[4096,16]{0,1:T(8,128)S(1)}, f32[4096,16]{0,1:T(8,128)}, u32[]{:S(2)}) copy-start(f32[4096,16]{0,1:T(8,128)} %param.8) | copy-start | bytes 786436
  3.8 0.9 %copy-start.3 = (f32[3,12288]{1,0:T(4,128)S(1)}, f32[3,12288]{1,0:T(4,128)}, u32[]{:S(2)}) copy-start(f32[3,12288]{1,0:T(4,128)} %taps.1) | copy-start | bytes 442372
  4.7 0.7 %copy-start.4 = (f32[4096]{0:T(1024)S(1)}, f32[4096]{0:T(1024)}, u32[]{:S(2)}) copy-start(f32[4096]{0:T(1024)} %param.9) | copy-start | bytes 49156
where the time goes:
time: 36.5 us; the launch traced here: 36.2 us
  Pallas kernels  29.8 us (82%)
  local copies, waits for them, and re-layouts  6.4 us (18%)
    pallas_call x1, Pallas kernels, per_device(): pl.pallas_call(functools.partial(kernel, n, rows, groups, modes), out_sha...  29.8 us
    unnamed x11, local copies, waits for them, and re-layouts  6.4 us

commit v1 on v0

v1 whole, which is shorter than its diff:
```python
import functools

import jax
import jax.numpy as jnp
from jax import lax
from jax.experimental import pallas as pl
from jax.experimental.pallas import tpu as pltpu
from jax.sharding import PartitionSpec as P

SHORT = 3
LANES = 128
SUB = 8
TILE = SUB * LANES
MESH = pl.DeviceIdType.MESH
F32 = jnp.float32
BF16 = jnp.bfloat16
WIRE = BF16
UNROLL = 7


def one_less_exp(x):
    series = x * (
        1.0
        - x * (1 / 2) * (1.0 - x * (1 / 3) * (1.0 - x * (1 / 4) * (1.0 - x * (1 / 5) * (1.0 - x * (1 / 6)))))
    )
    return jnp.where(x < 0.125, series, 1.0 - jnp.exp(-x))


def tree_sum(values):
    values = list(values)
    while len(values) > 1:
        paired = [values[k] + values[k + 1] for k in range(0, len(values) - 1, 2)]
        if len(values) % 2:
            paired.append(values[-1])
        values = paired
    return values[0]


def kernel(
    n, rows, groups, modes, owners,
    proj, taps_hbm, res_hbm, rate_hbm, skip_hbm, out,
    taps, res, rate, skip, small_sems,
    pin, rim_out, rim_in, px, z, y, first, pout, av, cv, tv,
    sent_f, sent, got, back, carry, carry_f,
    in_sems, out_sems, halo_send, halo_recv, send1, recv1, send2, recv2,
):
    me = lax.axis_index("context")
    tiles = groups // SUB
    per = groups // owners
    height = modes + 8

    barrier = pltpu.get_barrier_semaphore()

    def greet(k, c):
        pl.semaphore_signal(
            barrier, inc=1, device_id={"context": lax.rem(me + k, n)}, device_id_type=MESH
        )
        return c

    lax.fori_loop(1, n, greet, 0)

    small = [
        pltpu.make_async_copy(src, dst, small_sems.at[k])
        for k, (src, dst) in enumerate(
            [(rate_hbm, rate), (res_hbm, res), (taps_hbm, taps), (skip_hbm, skip)]
        )
    ]
    for copy in small:
        copy.start()

    def tile_copy(i):
        return pltpu.make_async_copy(
            proj.at[:, pl.ds(pl.multiple_of(i * TILE, TILE), TILE)], pin.at[i], in_sems.at[i]
        )

    def start_in(i, c):
        tile_copy(i).start()
        return c

    lax.fori_loop(tiles, 3 * tiles, start_in, 0)
    lax.fori_loop(0, tiles, start_in, 0)
    for copy in small:
        copy.wait()

    def params(j, c):
        cols = pl.ds(pl.multiple_of(j * LANES, LANES), LANES)
        r = rate[:, cols]
        where = pl.ds(j, modes, stride=groups)
        av[where, :] = jnp.exp(-r)
        cv[where, :] = res[:, cols] * jnp.sqrt(one_less_exp(2.0 * r))
        return c

    lax.fori_loop(0, groups, params, 0, unroll=4)

    def set_taps(j, c):
        cols = pl.ds(pl.multiple_of(j * LANES, LANES), LANES)
        tv[pl.ds(j, SHORT, stride=3 * groups), :] = taps[:, cols]
        return c

    lax.fori_loop(0, 3 * groups, set_taps, 0, unroll=8)

    def spread(i, c):
        tile_copy(i).wait()
        for j in range(SUB):
            px[i, pl.ds(2 * SUB + j, rows, stride=SUB), :] = pin[
                i, :, j * LANES : (j + 1) * LANES
            ].astype(F32)
        return c

    lax.fori_loop(tiles, 3 * tiles, spread, 0)

    def part(ref, m, i):
        return ref[pl.ds(pl.multiple_of(m * groups + i * SUB, SUB), SUB), :]

    def taps_of(stream, i):
        return [part(tv, 3 * k + stream, i) for k in range(SHORT)]

    def at(t):
        return pl.ds(pl.multiple_of(t * SUB, SUB), SUB)

    def token(stream, i, t):
        return px[stream * tiles + i, at(t + SHORT - 1), :]

    def pre(tap, stream, i, t):
        total = None
        for k in range(SHORT):
            term = tap[k] * token(stream, i, t - k)
            total = term if total is None else total + term
        return total

    def rounded(value):
        return value.astype(BF16).astype(F32)

    zeros = tuple(jnp.zeros((SUB, LANES), F32) for _ in range(modes))

    def end_states(i, c):
        a = [part(av, m, i) for m in range(modes)]
        tap2, tap3 = taps_of(1, i), taps_of(2, i)

        def step(t, h):
            zt = rounded(pre(tap2, 1, i, t) * pre(tap3, 2, i, t))
            z[i, at(t), :] = zt
            return tuple(a[m] * h[m] + zt for m in range(modes))

        h = lax.fori_loop(SHORT - 1, rows, step, zeros, unroll=UNROLL)
        edges = [token(s, i, t) for t in (0, 1, rows - 2, rows - 1) for s in (1, 2)]
        for m, value in enumerate(list(h) + edges):
            sent_f[pl.ds(i * SUB * height + m, SUB, stride=height), :] = value
        return c

    lax.fori_loop(0, tiles, end_states, 0)
    own = per * height
    for j in range(owners):
        sent[j, 0:own, :] = sent_f[j * own : (j + 1) * own, :].astype(WIRE)

    lax.fori_loop(0, tiles, spread, 0)
    for i in range(3 * tiles):
        rim_out[i * 16 : i * 16 + 16, :] = px[i, rows * SUB : (rows + 2) * SUB, :].astype(BF16)

    pl.semaphore_wait(barrier, n - 1)

    def send(src, dst, other, send_sem, recv_sem):
        pltpu.make_async_remote_copy(
            src_ref=src.at[other],
            dst_ref=dst.at[me],
            send_sem=send_sem,
            recv_sem=recv_sem,
            device_id={"context": other},
            device_id_type=MESH,
        ).start()

    def spend(ref, count, sem):
        most = pl.ds(0, count)
        pltpu.make_async_copy(ref.at[most], ref.at[most], sem).wait()

    def for_owner(body):
        if owners == n:
            body()
        else:
            pl.when(me < owners)(body)

    def for_other(body):
        if owners < n:
            pl.when(me >= owners)(body)

    def send_states(k, c):
        send(sent, got, lax.rem(me + k, owners), send1, recv1)
        return c

    @for_owner
    def _():
        lax.fori_loop(1, owners, send_states, 0)
        got[me] = sent[me]

    @for_other
    def _():
        lax.fori_loop(0, owners, send_states, 0)

    halo = pltpu.make_async_remote_copy(
        src_ref=rim_out,
        dst_ref=rim_in,
        send_sem=halo_send,
        recv_sem=halo_recv,
        device_id={"context": lax.rem(me + 1, n)},
        device_id_type=MESH,
    )

    @pl.when(me < n - 1)
    def _():
        halo.start()

    def local(i, c):
        a = [part(av, m, i) for m in range(modes)]
        coef = [part(cv, m, i) for m in range(modes)]
        direct = part(skip, 0, i)
        tap1 = taps_of(0, i)

        def step(t, h):
            zt = z[i, at(t), :]
            h = tuple(a[m] * h[m] + zt for m in range(modes))
            y[i, at(t), :] = direct * zt + tree_sum(coef[m] * h[m] for m in range(modes))
            first[i, at(t), :] = pre(tap1, 0, i, t)
            return h

        lax.fori_loop(SHORT - 1, rows, step, zeros, unroll=UNROLL)
        return c

    lax.fori_loop(0, tiles // 2, local, 0)

    @for_owner
    def _():
        spend(got, n - 1, recv1)
        decay, step1, late, tap2, tap3 = [], [], [], [], []
        for q in range(per):
            group = me * per + q
            r = rate[:, pl.ds(pl.multiple_of(group * LANES, LANES), LANES)]
            decay.append(jnp.exp(-float(rows) * r))
            late.append(jnp.exp(-float(rows - 2) * r))
            step1.append(jnp.exp(-r))
            for tap, stream in ((tap2, 1), (tap3, 2)):
                tap.append(
                    [tv[pl.ds((3 * k + stream) * groups + group, 1), :] for k in range(SHORT)]
                )

        def scan(d, held):
            block = got[d].astype(F32)
            following, returned = [], []
            for q in range(per):
                state, last = held[q]
                base = q * height
                edge = [block[base + modes + k : base + modes + k + 1] for k in range(8)]
                x0, v0, x1, v1 = edge[:4]
                xb, vb, xa, va = last

                def three(tap, now, before, ahead):
                    return tap[0] * now + tap[1] * before + tap[2] * ahead

                z0 = rounded(three(tap2[q], x0, xa, xb) * three(tap3[q], v0, va, vb))
                z1 = rounded(three(tap2[q], x1, x0, xa) * three(tap3[q], v1, v0, va))
                returned.append(state)
                state = (
                    decay[q] * state
                    + block[base : base + modes]
                    + late[q] * (step1[q] * z0 + z1)
                )
                following.append((state, tuple(edge[4:])))
            back[d] = jnp.concatenate(returned, axis=0).astype(WIRE)
            return tuple(following)

        none = tuple(jnp.zeros((1, LANES), F32) for _ in range(4))
        start = tuple((jnp.zeros((modes, LANES), F32), none) for _ in range(per))
        lax.fori_loop(0, n, scan, start, unroll=4)

        def send_back(k, c):
            send(back, carry, lax.rem(me + k, n), send2, recv2)
            return c

        lax.fori_loop(1, n, send_back, 0)
        carry[me] = back[me]

    lax.fori_loop(tiles // 2, tiles, local, 0)

    @pl.when(me < n - 1)
    def _():
        halo.wait_send()

    @pl.when(me > 0)
    def _():
        halo.wait_recv()

    @pl.when(me == 0)
    def _():
        rim_in[...] = jnp.zeros_like(rim_in)

    for i in range(3 * tiles):
        px[i, 0 : 2 * SUB, :] = rim_in[i * 16 : i * 16 + 16, :].astype(F32)

    @for_owner
    def _():
        spend(sent, owners - 1, send1)
        spend(back, n - 1, send2)
        spend(carry, owners - 1, recv2)

    @for_other
    def _():
        spend(sent, owners, send1)
        spend(carry, owners, recv2)

    for j in range(owners):
        carry_f[j * per * modes : (j + 1) * per * modes, :] = carry[j].astype(F32)

    def out_copy(i):
        return pltpu.make_async_copy(
            pout.at[i], out.at[:, pl.ds(pl.multiple_of(i * TILE, TILE), TILE)], out_sems.at[i]
        )

    def close(i, c):
        a = [part(av, m, i) for m in range(modes)]
        coef = [part(cv, m, i) for m in range(modes)]
        direct = part(skip, 0, i)
        tap1, tap2, tap3 = [taps_of(stream, i) for stream in range(3)]
        h = [carry_f[pl.ds(i * SUB * modes + m, SUB, stride=modes), :] for m in range(modes)]
        for t in range(SHORT - 1):
            zt = rounded(pre(tap2, 1, i, t) * pre(tap3, 2, i, t))
            h = [a[m] * h[m] + zt for m in range(modes)]
            mixed = rounded(direct * zt + tree_sum(coef[m] * h[m] for m in range(modes)))
            z[i, at(t), :] = pre(tap1, 0, i, t) * mixed
        g = tuple(coef[m] * h[m] for m in range(modes))

        def step(t, g):
            g = tuple(a[m] * g[m] for m in range(modes))
            mixed = rounded(y[i, at(t), :] + tree_sum(g))
            z[i, at(t), :] = first[i, at(t), :] * mixed
            return g

        lax.fori_loop(SHORT - 1, rows, step, g, unroll=UNROLL)
        for j in range(SUB):
            pout[i, :, j * LANES : (j + 1) * LANES] = z[
                i, pl.ds(j, rows, stride=SUB), :
            ].astype(BF16)
        out_copy(i).start()
        return c

    lax.fori_loop(0, tiles, close, 0)

    def end_out(i, c):
        out_copy(i).wait()
        return c

    lax.fori_loop(0, tiles, end_out, 0)


def per_device(projected, short_taps, residues, rates, skip):
    n = lax.axis_size("context")
    rows, width = projected.shape
    channels = width // 3
    modes = residues.shape[1]
    groups = channels // LANES
    tiles = channels // TILE
    owners = min(n, groups)
    per = groups // owners
    height = modes + 8
    padded = -(-per * height // 16) * 16
    hbm = pl.BlockSpec(memory_space=pl.ANY)
    dma = pltpu.SemaphoreType.DMA
    flat = pltpu.VMEM((modes * groups, LANES), F32)
    tokens = pltpu.VMEM((tiles, rows * SUB, LANES), F32)
    rims = pltpu.VMEM((3 * tiles * 16, LANES), BF16)
    return pl.pallas_call(
        functools.partial(kernel, n, rows, groups, modes, owners),
        out_shape=jax.ShapeDtypeStruct((rows, channels), BF16),
        in_specs=[hbm] * 5,
        out_specs=hbm,
        scratch_shapes=[
            pltpu.VMEM((SHORT, width), F32),
            pltpu.VMEM((modes, channels), F32),
            pltpu.VMEM((modes, channels), F32),
            pltpu.VMEM((groups, LANES), F32),
            dma((4,)),
            pltpu.VMEM((3 * tiles, rows, TILE), BF16),
            rims,
            rims,
            pltpu.VMEM((3 * tiles, (rows + 2) * SUB, LANES), F32),
            tokens,
            tokens,
            tokens,
            pltpu.VMEM((tiles, rows, TILE), BF16),
            flat,
            flat,
            pltpu.VMEM((SHORT * 3 * groups, LANES), F32),
            pltpu.VMEM((groups * height, LANES), F32),
            pltpu.VMEM((owners, padded, LANES), WIRE),
            pltpu.VMEM((n, padded, LANES), WIRE),
            pltpu.VMEM((n, per * modes, LANES), WIRE),
            pltpu.VMEM((owners, per * modes, LANES), WIRE),
            flat,
            dma((3 * tiles,)),
            dma((tiles,)),
            dma,
            dma,
            dma,
            dma,
            dma,
            dma,
        ],
        compiler_params=pltpu.CompilerParams(
            collective_id=0, has_side_effects=True, vmem_limit_bytes=60 * 1024 * 1024
        ),
        cost_estimate=pl.CostEstimate(
            flops=rows * channels * modes * 8, bytes_accessed=rows * channels * 8, transcendentals=0
        ),
    )(projected, short_taps, residues.T, rates.T, skip.reshape(groups, LANES))


def solution(mesh):
    in_specs = (P(("parts", "context"), None), P(), P(), P(), P())
    out_specs = P(("parts", "context"), None)
    return jax.shard_map(
        per_device, mesh=mesh, in_specs=in_specs, out_specs=out_specs, check_vma=False
    )
```

time: 36.5 us -> 27.4 us (0.75)
  Pallas kernels: 29.8 us -> 25 us
  local copies, waits for them, and re-layouts: 6.4 us -> 2.29 us
    pallas_call x1, Pallas kernels: 29.8 us -> 25 us  [per_device(): pl.pallas_call(functools.partial(kernel, n, rows, groups, modes, owners),...]
    unnamed x11 -> x1, local copies, waits for them, and re-layouts: 6.4 us -> 2.29 us
where the time goes in v1:
time: 27.4 us; the launch traced here: 27.3 us
  Pallas kernels  25 us (91%)
  local copies, waits for them, and re-layouts  2.29 us (8%)
    pallas_call x1, Pallas kernels, per_device(): pl.pallas_call(functools.partial(kernel, n, rows, groups, modes, owners),...  25 us
    unnamed x1, local copies, waits for them, and re-layouts  2.29 us

profile of v1, /device:TPU:0, one launch (start us, length us, event | category | flops | bytes accessed | tf_op | source)
XLA Modules:
  0.0 27.3 jit_solution(3845817801876746051)
XLA Ops:
  0.0 25.0 %shard_map.55 = bf16[128,4096]{1,0:T(8,128)(2,1)} custom-call(bf16[128,12288]{1,0:T(8,128)(2,1)} %proj.1, f32[3,12288]{1,0:T(4,128)} %taps_hbm.1, f32[16,4096]{1,0:T(8,128)} %bitcast.3, f32[16,4096]{1,0:T(8,128)} %bitcast.4, f32[32,128]{1,0:T(8,128)} %bitcast.5), custom_call_target="tpu_custom_call" | custom-call | flops 67108864 | bytes 4194304 | tf_op jit(solution)/shard_map/pallas_call | solution.py:369
  25.0 2.3 %copy.7 = bf16[128,4096]{1,0:T(8,128)(2,1)} copy(bf16[128,4096]{1,0:T(8,128)(2,1)} %shard_map.55) | data formatting | bytes 2097152

commit v2 on v1

--- a/solution.py
+++ b/solution.py
@@ -40,14 +40,20 @@
     n, rows, groups, modes, owners,
     proj, taps_hbm, res_hbm, rate_hbm, skip_hbm, out,
     taps, res, rate, skip, small_sems,
-    pin, rim_out, rim_in, px, z, y, first, pout, av, cv, tv,
+    pin, rim_out, rim_in, px, z, y, first, av, cv, tv,
     sent_f, sent, got, back, carry, carry_f,
-    in_sems, out_sems, halo_send, halo_recv, send1, recv1, send2, recv2,
+    in_sems, halo_send, halo_recv, send1, recv1, send2, recv2,
 ):
     me = lax.axis_index("context")
     tiles = groups // SUB
     per = groups // owners
     height = modes + 8
+    own = per * height
+    crew = SUB // per
+    home = lax.rem(me, owners) // crew
+
+    def turn(k):
+        return lax.rem(home + k, tiles)
 
     barrier = pltpu.get_barrier_semaphore()
 
@@ -62,11 +68,11 @@
     small = [
         pltpu.make_async_copy(src, dst, small_sems.at[k])
         for k, (src, dst) in enumerate(
-            [(rate_hbm, rate), (res_hbm, res), (taps_hbm, taps), (skip_hbm, skip)]
+            [(rate_hbm, rate), (taps_hbm, taps), (res_hbm, res), (skip_hbm, skip)]
         )
     ]
-    for copy in small:
-        copy.start()
+    small[0].start()
+    small[1].start()
 
     def tile_copy(i):
         return pltpu.make_async_copy(
@@ -77,17 +83,18 @@
         tile_copy(i).start()
         return c
 
-    lax.fori_loop(tiles, 3 * tiles, start_in, 0)
+    for k in range(1, tiles + 1):
+        tile_copy(tiles + turn(k)).start()
+        tile_copy(2 * tiles + turn(k)).start()
     lax.fori_loop(0, tiles, start_in, 0)
-    for copy in small:
-        copy.wait()
+    small[2].start()
+    small[3].start()
+    small[0].wait()
+    small[1].wait()
 
     def params(j, c):
         cols = pl.ds(pl.multiple_of(j * LANES, LANES), LANES)
-        r = rate[:, cols]
-        where = pl.ds(j, modes, stride=groups)
-        av[where, :] = jnp.exp(-r)
-        cv[where, :] = res[:, cols] * jnp.sqrt(one_less_exp(2.0 * r))
+        av[pl.ds(j, modes, stride=groups), :] = jnp.exp(-rate[:, cols])
         return c
 
     lax.fori_loop(0, groups, params, 0, unroll=4)
@@ -107,7 +114,6 @@
             ].astype(F32)
         return c
 
-    lax.fori_loop(tiles, 3 * tiles, spread, 0)
 
     def part(ref, m, i):
         return ref[pl.ds(pl.multiple_of(m * groups + i * SUB, SUB), SUB), :]
@@ -133,7 +139,9 @@
 
     zeros = tuple(jnp.zeros((SUB, LANES), F32) for _ in range(modes))
 
-    def end_states(i, c):
+    def end_states(i):
+        spread(tiles + i, 0)
+        spread(2 * tiles + i, 0)
         a = [part(av, m, i) for m in range(modes)]
         tap2, tap3 = taps_of(1, i), taps_of(2, i)
 
@@ -146,18 +154,9 @@
         edges = [token(s, i, t) for t in (0, 1, rows - 2, rows - 1) for s in (1, 2)]
         for m, value in enumerate(list(h) + edges):
             sent_f[pl.ds(i * SUB * height + m, SUB, stride=height), :] = value
-        return c
-
-    lax.fori_loop(0, tiles, end_states, 0)
-    own = per * height
-    for j in range(owners):
-        sent[j, 0:own, :] = sent_f[j * own : (j + 1) * own, :].astype(WIRE)
-
-    lax.fori_loop(0, tiles, spread, 0)
-    for i in range(3 * tiles):
-        rim_out[i * 16 : i * 16 + 16, :] = px[i, rows * SUB : (rows + 2) * SUB, :].astype(BF16)
-
-    pl.semaphore_wait(barrier, n - 1)
+        for k in range(crew):
+            j = i * crew + k
+            sent[j, 0:own, :] = sent_f[pl.ds(pl.multiple_of(j * own, SUB), own), :].astype(WIRE)
 
     def send(src, dst, other, send_sem, recv_sem):
         pltpu.make_async_remote_copy(
@@ -183,18 +182,31 @@
         if owners < n:
             pl.when(me >= owners)(body)
 
-    def send_states(k, c):
-        send(sent, got, lax.rem(me + k, owners), send1, recv1)
-        return c
+    def ship(i):
+        for k in range(crew):
+            j = i * crew + k
+
+            @pl.when(j != me)
+            def _():
+                send(sent, got, j, send1, recv1)
+
+    def pass_tile(k, c):
+        end_states(turn(k))
+        ship(turn(k))
+        return c
+
+    end_states(turn(1))
+    pl.semaphore_wait(barrier, n - 1)
+    ship(turn(1))
+    lax.fori_loop(2, tiles + 1, pass_tile, 0)
 
     @for_owner
     def _():
-        lax.fori_loop(1, owners, send_states, 0)
         got[me] = sent[me]
 
-    @for_other
-    def _():
-        lax.fori_loop(0, owners, send_states, 0)
+    lax.fori_loop(0, tiles, spread, 0)
+    for i in range(3 * tiles):
+        rim_out[i * 16 : i * 16 + 16, :] = px[i, rows * SUB : (rows + 2) * SUB, :].astype(BF16)
 
     halo = pltpu.make_async_remote_copy(
         src_ref=rim_out,
@@ -208,6 +220,18 @@
     @pl.when(me < n - 1)
     def _():
         halo.start()
+
+    small[2].wait()
+    small[3].wait()
+
+    def coefs(j, c):
+        cols = pl.ds(pl.multiple_of(j * LANES, LANES), LANES)
+        cv[pl.ds(j, modes, stride=groups), :] = res[:, cols] * jnp.sqrt(
+            one_less_exp(2.0 * rate[:, cols])
+        )
+        return c
+
+    lax.fori_loop(0, groups, coefs, 0, unroll=4)
 
     def local(i, c):
         a = [part(av, m, i) for m in range(modes)]
@@ -272,7 +296,7 @@
         lax.fori_loop(0, n, scan, start, unroll=4)
 
         def send_back(k, c):
-            send(back, carry, lax.rem(me + k, n), send2, recv2)
+            send(back, carry, lax.rem(me + k, n), send2, recv2.at[home])
             return c
 
         lax.fori_loop(1, n, send_back, 0)
@@ -295,26 +319,22 @@
     for i in range(3 * tiles):
         px[i, 0 : 2 * SUB, :] = rim_in[i * 16 : i * 16 + 16, :].astype(F32)
 
-    @for_owner
-    def _():
-        spend(sent, owners - 1, send1)
-        spend(back, n - 1, send2)
-        spend(carry, owners - 1, recv2)
-
-    @for_other
-    def _():
-        spend(sent, owners, send1)
-        spend(carry, owners, recv2)
-
-    for j in range(owners):
-        carry_f[j * per * modes : (j + 1) * per * modes, :] = carry[j].astype(F32)
-
-    def out_copy(i):
-        return pltpu.make_async_copy(
-            pout.at[i], out.at[:, pl.ds(pl.multiple_of(i * TILE, TILE), TILE)], out_sems.at[i]
-        )
-
-    def close(i, c):
+    def close(k, c):
+        i = turn(k)
+
+        @pl.when(jnp.logical_and(k == 0, me < owners))
+        def _():
+            spend(carry, crew - 1, recv2.at[i])
+
+        @pl.when(jnp.logical_or(k > 0, me >= owners))
+        def _():
+            spend(carry, crew, recv2.at[i])
+
+        for j in range(crew):
+            chunk = per * modes
+            carry_f[pl.ds(pl.multiple_of((i * crew + j) * chunk, SUB), chunk), :] = carry[
+                i * crew + j
+            ].astype(F32)
         a = [part(av, m, i) for m in range(modes)]
         coef = [part(cv, m, i) for m in range(modes)]
         direct = part(skip, 0, i)
@@ -335,19 +355,22 @@
 
         lax.fori_loop(SHORT - 1, rows, step, g, unroll=UNROLL)
         for j in range(SUB):
-            pout[i, :, j * LANES : (j + 1) * LANES] = z[
+            cols = pl.ds(pl.multiple_of(i * TILE + j * LANES, LANES), LANES)
+            out[:, cols] = z[
                 i, pl.ds(j, rows, stride=SUB), :
             ].astype(BF16)
-        out_copy(i).start()
         return c
 
     lax.fori_loop(0, tiles, close, 0)
 
-    def end_out(i, c):
-        out_copy(i).wait()
-        return c
-
-    lax.fori_loop(0, tiles, end_out, 0)
+    @for_owner
+    def _():
+        spend(sent, owners - 1, send1)
+        spend(back, n - 1, send2)
+
+    @for_other
+    def _():
+        spend(sent, owners, send1)
 
 
 def per_device(projected, short_taps, residues, rates, skip):
@@ -368,9 +391,9 @@
     rims = pltpu.VMEM((3 * tiles * 16, LANES), BF16)
     return pl.pallas_call(
         functools.partial(kernel, n, rows, groups, modes, owners),
-        out_shape=jax.ShapeDtypeStruct((rows, channels), BF16),
+        out_shape=pltpu.VMEM((rows, channels), BF16),
         in_specs=[hbm] * 5,
-        out_specs=hbm,
+        out_specs=pl.BlockSpec(memory_space=pltpu.VMEM),
         scratch_shapes=[
             pltpu.VMEM((SHORT, width), F32),
             pltpu.VMEM((modes, channels), F32),
@@ -384,7 +407,6 @@
             tokens,
             tokens,
             tokens,
-            pltpu.VMEM((tiles, rows, TILE), BF16),
             flat,
             flat,
             pltpu.VMEM((SHORT * 3 * groups, LANES), F32),
@@ -395,13 +417,12 @@
             pltpu.VMEM((owners, per * modes, LANES), WIRE),
             flat,
             dma((3 * tiles,)),
-            dma((tiles,)),
             dma,
             dma,
             dma,
             dma,
             dma,
-            dma,
+            dma((tiles,)),
         ],
         compiler_params=pltpu.CompilerParams(
             collective_id=0, has_side_effects=True, vmem_limit_bytes=60 * 1024 * 1024

time: 27.4 us -> 21.6 us (0.79)
  Pallas kernels: 25 us -> 20.5 us
  local copies, waits for them, and re-layouts: 2.29 us -> 0.97 us
    pallas_call x1, Pallas kernels: 25 us -> 20.5 us  [per_device(): pl.pallas_call(functools.partial(kernel, n, rows, groups, modes, owners),...]
    unnamed x1, local copies, waits for them, and re-layouts: 2.29 us -> 0.97 us
where the time goes in v2:
time: 21.6 us; the launch traced here: 21.4 us
  Pallas kernels  20.5 us (95%)
  local copies, waits for them, and re-layouts  0.97 us (4%)
    pallas_call x1, Pallas kernels, per_device(): pl.pallas_call(functools.partial(kernel, n, rows, groups, modes, owners),...  20.5 us
    unnamed x1, local copies, waits for them, and re-layouts  0.97 us

profile of v2, /device:TPU:0, one launch (start us, length us, event | category | flops | bytes accessed | tf_op | source)
XLA Modules:
  0.0 21.4 jit_solution(3694364293667206438)
XLA Ops:
  0.0 20.5 %shard_map.55 = bf16[128,4096]{1,0:T(8,128)(2,1)S(1)} custom-call(bf16[128,12288]{1,0:T(8,128)(2,1)} %proj.1, f32[3,12288]{1,0:T(4,128)} %taps_hbm.1, f32[16,4096]{1,0:T(8,128)} %bitcast.3, f32[16,4096]{1,0:T(8,128)} %bitcast.4, f32[32,128]{1,0:T(8,128)} %bitcast.5), custom_call_target="tpu_custom_call" | custom-call | flops 67108864 | bytes 4194304 | tf_op jit(solution)/shard_map/pallas_call | solution.py:392
  20.5 1.0 %copy.7 = bf16[128,4096]{1,0:T(8,128)(2,1)} copy(bf16[128,4096]{1,0:T(8,128)(2,1)S(1)} %shard_map.55) | data formatting | bytes 2097152

commit v3 on v2

--- a/solution.py
+++ b/solution.py
@@ -15,7 +15,7 @@
 F32 = jnp.float32
 BF16 = jnp.bfloat16
 WIRE = BF16
-UNROLL = 7
+UNROLL = 14
 
 
 def one_less_exp(x):
@@ -104,7 +104,7 @@
         tv[pl.ds(j, SHORT, stride=3 * groups), :] = taps[:, cols]
         return c
 
-    lax.fori_loop(0, 3 * groups, set_taps, 0, unroll=8)
+    lax.fori_loop(groups, 3 * groups, set_taps, 0, unroll=8)
 
     def spread(i, c):
         tile_copy(i).wait()
@@ -232,6 +232,7 @@
         return c
 
     lax.fori_loop(0, groups, coefs, 0, unroll=4)
+    lax.fori_loop(0, groups, set_taps, 0, unroll=8)
 
     def local(i, c):
         a = [part(av, m, i) for m in range(modes)]

time: 21.6 us -> 21.2 us (0.981)
  Pallas kernels: 20.5 us -> 20.1 us
    pallas_call x1, Pallas kernels: 20.5 us -> 20.1 us  [per_device(): pl.pallas_call(functools.partial(kernel, n, rows, groups, modes, owners),...]
where the time goes in v3:
time: 21.2 us; the launch traced here: 21.1 us
  Pallas kernels  20.1 us (95%)
  local copies, waits for them, and re-layouts  0.97 us (5%)
    pallas_call x1, Pallas kernels, per_device(): pl.pallas_call(functools.partial(kernel, n, rows, groups, modes, owners),...  20.1 us
    unnamed x1, local copies, waits for them, and re-layouts  0.97 us

profile of v3, /device:TPU:0, one launch (start us, length us, event | category | flops | bytes accessed | tf_op | source)
XLA Modules:
  0.0 21.1 jit_solution(1941192209497596072)
XLA Ops:
  0.0 20.1 %shard_map.55 = bf16[128,4096]{1,0:T(8,128)(2,1)S(1)} custom-call(bf16[128,12288]{1,0:T(8,128)(2,1)} %proj.1, f32[3,12288]{1,0:T(4,128)} %taps_hbm.1, f32[16,4096]{1,0:T(8,128)} %bitcast.3, f32[16,4096]{1,0:T(8,128)} %bitcast.4, f32[32,128]{1,0:T(8,128)} %bitcast.5), custom_call_target="tpu_custom_call" | custom-call | flops 67108864 | bytes 4194304 | tf_op jit(solution)/shard_map/pallas_call | solution.py:393
  20.1 1.0 %copy.7 = bf16[128,4096]{1,0:T(8,128)(2,1)} copy(bf16[128,4096]{1,0:T(8,128)(2,1)S(1)} %shard_map.55) | data formatting | bytes 2097152
